TPU v7x, 1024 devices: a whole 4x8x16 slice. The times are simulated.
1024 devices in a mesh: ctx: 256 (over z, y, core), tp: 4 (over x).
Axes of the slice: x: 4, y: 8, z: 16, core: 2. Of those that a mesh axis runs over, the one named last changes fastest.
Arguments:
- key_value: bfloat16 [65536, 4, 256], P('ctx', 'tp'), may hold values from -6 to 6
- queries: bfloat16 [65536, 32, 128], P('ctx', 'tp')
- doc_lengths: int32 [128], replicated, may hold values from 1 to 1024, 65536 in all
Outputs:
- attended: bfloat16 [65536, 32, 128], P('ctx', 'tp')
Inputs may be any that keep to these rules, and one draw needn't show every extreme that they name: `doc_lengths`: the lengths sum to 65536 and the longest is exactly 1024.
All inputs are finite; a program needn't handle non-finite values.
Results may differ from a plain program's by a relative error of at most 0.017.
The roundings to bfloat16 on the way count: a program that leaves them out, or rounds other values in their place, can miss the bound.
Values may be sent and summed in bfloat16 or wider, within the bound.
A program may use at most 32 MiB of HBM per device.

v0:
```python
import math

import jax
import jax.numpy as jnp
from jax import lax
from jax.sharding import PartitionSpec as P

WINDOW = 8


ROPE_BASE = 500000.0
MASKED = -1e30


def from_behind(value, axis, steps):
    count = lax.axis_size(axis)
    leading, last = (max(0, -steps), min(count, count - steps))
    return lax.ppermute(value, axis, [(source, source + steps) for source in range(leading, last)])


def rotate(vectors, positions):
    width = vectors.shape[-1]
    half = width // 2
    inverse_freq = ROPE_BASE ** (-(jnp.arange(half, dtype=jnp.float32) * 2.0 / width))
    angles = positions.astype(jnp.float32)[..., None] * inverse_freq
    cosine = jnp.cos(angles)[..., None, :]
    sine_part = jnp.sin(angles)[..., None, :]
    front_half = vectors[..., :half]
    back_half = vectors[..., half:]
    return jnp.concatenate(
        [front_half * cosine - back_half * sine_part, back_half * cosine + front_half * sine_part],
        axis=-1,
    )


def shards(key_value, queries, doc_lengths):
    rows = key_value.shape[0]
    kv_heads = key_value.shape[1]
    pair_width = key_value.shape[2]
    head_size = queries.shape[-1]
    q_heads = queries.shape[1]
    group_size = q_heads // kv_heads
    half_rows = rows // 2
    score_scale = 1.0 / math.sqrt(head_size)
    devices = lax.axis_size("ctx")
    my_index = lax.axis_index("ctx")
    doc_ends = jnp.cumsum(doc_lengths)
    offsets = jnp.arange(half_rows, dtype=jnp.int32)

    def locate(block_ids):
        place = block_ids[:, None] * half_rows + offsets[None, :]
        document = jnp.sum((place[:, :, None] >= doc_ends[None, None, :]).astype(jnp.int32), axis=2)
        return (place, document)

    own_blocks = jnp.stack([my_index, 2 * devices - 1 - my_index])
    own_place, own_doc = locate(own_blocks)
    pairs = key_value.reshape(2, half_rows, kv_heads, pair_width)
    rotated_kv = jnp.concatenate(
        [
            rotate(pairs[..., :head_size].astype(jnp.float32), own_place),
            pairs[..., head_size:].astype(jnp.float32),
        ],
        axis=-1,
    ).astype(jnp.bfloat16)
    rotated = (
        rotate(queries.reshape(2, half_rows, q_heads, head_size).astype(jnp.float32), own_place)
        .astype(jnp.bfloat16)
        .reshape(2, half_rows, kv_heads, group_size, head_size)
    )

    def attend(carry, key_block, key_blocks):
        running_max, running_sum, running_out = carry
        key_place, key_doc = locate(key_blocks)
        allowed = (
            (key_doc[:, None, :] == own_doc[:, :, None])
            & (key_place[:, None, :] <= own_place[:, :, None])
            & (key_blocks >= 0)[:, None, None]
        )
        scores = (
            jnp.einsum(
                "sthgc,snhc->sthgn",
                rotated,
                key_block[..., :head_size],
                preferred_element_type=jnp.float32,
            )
            * score_scale
        )
        visible = allowed[:, :, None, None, :]
        block_max = jnp.max(jnp.where(visible, scores, MASKED), axis=-1)
        new_max = jnp.maximum(running_max, block_max)
        weights = jnp.where(visible, jnp.exp(scores - new_max[..., None]), 0.0)
        factor = jnp.exp(running_max - new_max)
        new_sum = running_sum * factor + jnp.sum(weights, axis=-1)
        rounded_weights = weights.astype(jnp.bfloat16)
        new_out = running_out * factor[..., None] + jnp.einsum(
            "sthgn,snhc->sthgc",
            rounded_weights,
            key_block[..., head_size:],
            preferred_element_type=jnp.float32,
        )
        return (new_max, new_sum, new_out)

    initial = (
        jnp.full((2, half_rows, kv_heads, group_size), MASKED, jnp.float32),
        jnp.zeros((2, half_rows, kv_heads, group_size), jnp.float32),
        jnp.zeros((2, half_rows, kv_heads, group_size, head_size), jnp.float32),
    )
    carry = attend(initial, rotated_kv, own_blocks)
    at_fold = my_index == devices - 1
    stream = rotated_kv
    for step in range(1, WINDOW + 1):
        rising = from_behind(stream[0], "ctx", 1)
        falling = from_behind(stream[1], "ctx", -1)
        falling = jnp.where(at_fold, stream[0], falling)
        stream = jnp.stack([rising, falling])
        carry = attend(carry, stream, own_blocks - step)
    result = carry[2] / carry[1][..., None]
    return result.reshape(rows, q_heads, head_size).astype(jnp.bfloat16)


def solution(mesh):
    in_specs = (P("ctx", "tp", None), P("ctx", "tp", None), P())
    out_specs = P("ctx", "tp", None)
    return jax.shard_map(shards, mesh=mesh, in_specs=in_specs, out_specs=out_specs, check_vma=False)
```

profile of v0, /device:TPU:770, one launch (start us, length us, event | category | flops | bytes accessed | tf_op | source)
XLA Modules:
  0.0 94.3 jit_solution(17191638599242520416)
XLA Ops:
  0.2 0.9 fusion.183
  1.1 0.6 fusion.97
  1.8 2.1 %collective-permute-start = (bf16[128,1,256]{2,0,1:T(8,128)(2,1)S(1)}, bf16[128,1,256]{2,0,1:T(8,128)(2,1)S(1)}, u32[]{:S(2)}, u32[]{:S(2)}) collective-permute-start(bf16[128,1,256]{2,0,1:T(8,128)(2,1)S(1)} %slice_bitcast_fusion.1), channel_id=1, source_target_pairs={{0,4},{4,8},{8,12},{12,16},{16,20},{20,24},{24,28},{28,32},{32,36}... | collective-permute-start | bytes 196616 | tf_op jit(solution)/shard_map/ppermute | solution.py:18
  4.0 7.0 %collective-permute-start.1 = (bf16[128,1,256]{2,0,1:T(8,128)(2,1)S(1)}, bf16[128,1,256]{2,0,1:T(8,128)(2,1)S(1)}, u32[]{:S(2)}, u32[]{:S(2)}) collective-permute-start(bf16[128,1,256]{2,0,1:T(8,128)(2,1)S(1)} %slice_bitcast_fusion), channel_id=1, source_target_pairs={{4,0},{8,4},{12,8},{16,12},{20,16},{24,20},{28,24},{32,28},{36,32}... | collective-permute-start | bytes 196616 | tf_op jit(solution)/shard_map/ppermute | solution.py:18
  11.5 0.6 copy-done.2
  14.3 0.6 and_and_fusion.8
  15.4 4.5 %collective-permute-start.3 = (bf16[128,1,256]{2,0,1:T(8,128)(2,1)S(1)}, bf16[128,1,256]{2,0,1:T(8,128)(2,1)S(1)}, u32[]{:S(2)}, u32[]{:S(2)}) collective-permute-start(bf16[128,1,256]{2,0,1:T(8,128)(2,1)S(1)} %broadcast_select_fusion.6), channel_id=1, source_target_pairs={{4,0},{8,4},{12,8},{16,12},{20,16},{24,20},{28,24},{32,28},{36,32}... | collective-permute-start | bytes 196616 | tf_op jit(solution)/shard_map/ppermute | solution.py:18
  20.2 1.9 %collective-permute-start.2 = (bf16[128,1,256]{2,0,1:T(8,128)(2,1)S(1)}, bf16[128,1,256]{2,0,1:T(8,128)(2,1)S(1)}, u32[]{:S(2)}, u32[]{:S(2)}) collective-permute-start(bf16[128,1,256]{2,0,1:T(8,128)(2,1)S(1)} %collective-permute-done), channel_id=1, source_target_pairs={{0,4},{4,8},{8,12},{12,16},{16,20},{20,24},{24,28},{28,32},{32,36}... | collective-permute-start | bytes 196616 | tf_op jit(solution)/shard_map/ppermute | solution.py:18
  22.2 7.0 %collective-permute-start.5 = (bf16[128,1,256]{2,0,1:T(8,128)(2,1)S(1)}, bf16[128,1,256]{2,0,1:T(8,128)(2,1)S(1)}, u32[]{:S(2)}, u32[]{:S(2)}) collective-permute-start(bf16[128,1,256]{2,0,1:T(8,128)(2,1)S(1)} %broadcast_select_fusion.5), channel_id=1, source_target_pairs={{4,0},{8,4},{12,8},{16,12},{20,16},{24,20},{28,24},{32,28},{36,32}... | collective-permute-start | bytes 196616 | tf_op jit(solution)/shard_map/ppermute | solution.py:18
  29.5 1.9 %collective-permute-start.4 = (bf16[128,1,256]{2,0,1:T(8,128)(2,1)S(1)}, bf16[128,1,256]{2,0,1:T(8,128)(2,1)S(1)}, u32[]{:S(2)}, u32[]{:S(2)}) collective-permute-start(bf16[128,1,256]{2,0,1:T(8,128)(2,1)S(1)} %collective-permute-done.2), channel_id=1, source_target_pairs={{0,4},{4,8},{8,12},{12,16},{16,20},{20,24},{24,28},{28,32},{32,36}... | collective-permute-start | bytes 196616 | tf_op jit(solution)/shard_map/ppermute | solution.py:18
  31.4 7.0 %collective-permute-start.7 = (bf16[128,1,256]{2,0,1:T(8,128)(2,1)S(1)}, bf16[128,1,256]{2,0,1:T(8,128)(2,1)S(1)}, u32[]{:S(2)}, u32[]{:S(2)}) collective-permute-start(bf16[128,1,256]{2,0,1:T(8,128)(2,1)S(1)} %broadcast_select_fusion.4), channel_id=1, source_target_pairs={{4,0},{8,4},{12,8},{16,12},{20,16},{24,20},{28,24},{32,28},{36,32}... | collective-permute-start | bytes 196616 | tf_op jit(solution)/shard_map/ppermute | solution.py:18
  38.7 1.9 %collective-permute-start.6 = (bf16[128,1,256]{2,0,1:T(8,128)(2,1)S(1)}, bf16[128,1,256]{2,0,1:T(8,128)(2,1)S(1)}, u32[]{:S(2)}, u32[]{:S(2)}) collective-permute-start(bf16[128,1,256]{2,0,1:T(8,128)(2,1)S(1)} %collective-permute-done.4), channel_id=1, source_target_pairs={{0,4},{4,8},{8,12},{12,16},{16,20},{20,24},{24,28},{28,32},{32,36}... | collective-permute-start | bytes 196616 | tf_op jit(solution)/shard_map/ppermute | solution.py:18
  40.7 7.0 %collective-permute-start.9 = (bf16[128,1,256]{2,0,1:T(8,128)(2,1)S(1)}, bf16[128,1,256]{2,0,1:T(8,128)(2,1)S(1)}, u32[]{:S(2)}, u32[]{:S(2)}) collective-permute-start(bf16[128,1,256]{2,0,1:T(8,128)(2,1)S(1)} %broadcast_select_fusion.3), channel_id=1, source_target_pairs={{4,0},{8,4},{12,8},{16,12},{20,16},{24,20},{28,24},{32,28},{36,32}... | collective-permute-start | bytes 196616 | tf_op jit(solution)/shard_map/ppermute | solution.py:18
  48.0 1.9 %collective-permute-start.8 = (bf16[128,1,256]{2,0,1:T(8,128)(2,1)S(1)}, bf16[128,1,256]{2,0,1:T(8,128)(2,1)S(1)}, u32[]{:S(2)}, u32[]{:S(2)}) collective-permute-start(bf16[128,1,256]{2,0,1:T(8,128)(2,1)S(1)} %collective-permute-done.6), channel_id=1, source_target_pairs={{0,4},{4,8},{8,12},{12,16},{16,20},{20,24},{24,28},{28,32},{32,36}... | collective-permute-start | bytes 196616 | tf_op jit(solution)/shard_map/ppermute | solution.py:18
  49.9 7.0 %collective-permute-start.11 = (bf16[128,1,256]{2,0,1:T(8,128)(2,1)S(1)}, bf16[128,1,256]{2,0,1:T(8,128)(2,1)S(1)}, u32[]{:S(2)}, u32[]{:S(2)}) collective-permute-start(bf16[128,1,256]{2,0,1:T(8,128)(2,1)S(1)} %broadcast_select_fusion.2), channel_id=1, source_target_pairs={{4,0},{8,4},{12,8},{16,12},{20,16},{24,20},{28,24},{32,28},{36,32}... | collective-permute-start | bytes 196616 | tf_op jit(solution)/shard_map/ppermute | solution.py:18
  57.2 1.9 %collective-permute-start.10 = (bf16[128,1,256]{2,0,1:T(8,128)(2,1)S(1)}, bf16[128,1,256]{2,0,1:T(8,128)(2,1)S(1)}, u32[]{:S(2)}, u32[]{:S(2)}) collective-permute-start(bf16[128,1,256]{2,0,1:T(8,128)(2,1)S(1)} %collective-permute-done.8), channel_id=1, source_target_pairs={{0,4},{4,8},{8,12},{12,16},{16,20},{20,24},{24,28},{28,32},{32,36}... | collective-permute-start | bytes 196616 | tf_op jit(solution)/shard_map/ppermute | solution.py:18
  59.2 7.0 %collective-permute-start.13 = (bf16[128,1,256]{2,0,1:T(8,128)(2,1)S(1)}, bf16[128,1,256]{2,0,1:T(8,128)(2,1)S(1)}, u32[]{:S(2)}, u32[]{:S(2)}) collective-permute-start(bf16[128,1,256]{2,0,1:T(8,128)(2,1)S(1)} %broadcast_select_fusion.1), channel_id=1, source_target_pairs={{4,0},{8,4},{12,8},{16,12},{20,16},{24,20},{28,24},{32,28},{36,32}... | collective-permute-start | bytes 196616 | tf_op jit(solution)/shard_map/ppermute | solution.py:18
  66.5 1.9 %collective-permute-start.12 = (bf16[128,1,256]{2,0,1:T(8,128)(2,1)S(1)}, bf16[128,1,256]{2,0,1:T(8,128)(2,1)S(1)}, u32[]{:S(2)}, u32[]{:S(2)}) collective-permute-start(bf16[128,1,256]{2,0,1:T(8,128)(2,1)S(1)} %collective-permute-done.10), channel_id=1, source_target_pairs={{0,4},{4,8},{8,12},{12,16},{16,20},{20,24},{24,28},{28,32},{32,36}... | collective-permute-start | bytes 196616 | tf_op jit(solution)/shard_map/ppermute | solution.py:18
  68.5 7.0 %collective-permute-start.15 = (bf16[128,1,256]{2,0,1:T(8,128)(2,1)S(1)}, bf16[128,1,256]{2,0,1:T(8,128)(2,1)S(1)}, u32[]{:S(2)}, u32[]{:S(2)}) collective-permute-start(bf16[128,1,256]{2,0,1:T(8,128)(2,1)S(1)} %broadcast_select_fusion), channel_id=1, source_target_pairs={{4,0},{8,4},{12,8},{16,12},{20,16},{24,20},{28,24},{32,28},{36,32}... | collective-permute-start | bytes 196616 | tf_op jit(solution)/shard_map/ppermute | solution.py:18
  75.8 2.1 %collective-permute-start.14 = (bf16[128,1,256]{2,0,1:T(8,128)(2,1)S(1)}, bf16[128,1,256]{2,0,1:T(8,128)(2,1)S(1)}, u32[]{:S(2)}, u32[]{:S(2)}) collective-permute-start(bf16[128,1,256]{2,0,1:T(8,128)(2,1)S(1)} %collective-permute-done.12), channel_id=1, source_target_pairs={{0,4},{4,8},{8,12},{12,16},{16,20},{20,24},{24,28},{28,32},{32,36}... | collective-permute-start | bytes 196616 | tf_op jit(solution)/shard_map/ppermute | solution.py:18
  77.9 6.8 %collective-permute-done.14 = bf16[128,1,256]{2,0,1:T(8,128)(2,1)S(1)} collective-permute-done((bf16[128,1,256]{2,0,1:T(8,128)(2,1)S(1)}, bf16[128,1,256]{2,0,1:T(8,128)(2,1)S(1)}, u32[]{:S(2)}, u32[]{:S(2)}) %collective-permute-start.14) | collective-permute-done | bytes 65568 | tf_op jit(solution)/shard_map/ppermute | solution.py:18
  87.0 0.9 copy-done.1
  87.8 0.9 fusion.10
  93.1 1.1 %copy.28 = bf16[2,128,1,8,128]{4,3,1,0,2:T(8,128)(2,1)} copy(bf16[2,128,1,8,128]{4,1,3,0,2:T(8,128)(2,1)S(1)} %fusion.28) | data formatting | bytes 1048576 | tf_op jit(solution)/shard_map/convert_element_type | solution.py:118
  (77 shorter events, 12.4 us)
Async XLA Ops:
  1.8 10.8 %copy-start = (bf16[256,8,128]{2,1,0:T(8,128)(2,1)S(1)}, bf16[256,8,128]{2,1,0:T(8,128)(2,1)}, u32[]{:S(2)}) copy-start(bf16[256,8,128]{2,1,0:T(8,128)(2,1)} %param.4) | copy-start | bytes 1572868
  1.8 18.1 %collective-permute-start = (bf16[128,1,256]{2,0,1:T(8,128)(2,1)S(1)}, bf16[128,1,256]{2,0,1:T(8,128)(2,1)S(1)}, u32[]{:S(2)}, u32[]{:S(2)}) collective-permute-start(bf16[128,1,256]{2,0,1:T(8,128)(2,1)S(1)} %slice_bitcast_fusion.1), channel_id=1, source_target_pairs={{0,4},{4,8},{8,12},{12,16},{16,20},{20,24},{24,28},{28,32},{32,36}... | collective-permute-start | bytes 196616 | tf_op jit(solution)/shard_map/ppermute | solution.py:18
  4.0 11.4 %collective-permute-start.1 = (bf16[128,1,256]{2,0,1:T(8,128)(2,1)S(1)}, bf16[128,1,256]{2,0,1:T(8,128)(2,1)S(1)}, u32[]{:S(2)}, u32[]{:S(2)}) collective-permute-start(bf16[128,1,256]{2,0,1:T(8,128)(2,1)S(1)} %slice_bitcast_fusion), channel_id=1, source_target_pairs={{4,0},{8,4},{12,8},{16,12},{20,16},{24,20},{28,24},{32,28},{36,32}... | collective-permute-start | bytes 196616 | tf_op jit(solution)/shard_map/ppermute | solution.py:18
  11.5 0.7 copy-start.2
  15.4 6.8 %collective-permute-start.3 = (bf16[128,1,256]{2,0,1:T(8,128)(2,1)S(1)}, bf16[128,1,256]{2,0,1:T(8,128)(2,1)S(1)}, u32[]{:S(2)}, u32[]{:S(2)}) collective-permute-start(bf16[128,1,256]{2,0,1:T(8,128)(2,1)S(1)} %broadcast_select_fusion.6), channel_id=1, source_target_pairs={{4,0},{8,4},{12,8},{16,12},{20,16},{24,20},{28,24},{32,28},{36,32}... | collective-permute-start | bytes 196616 | tf_op jit(solution)/shard_map/ppermute | solution.py:18
  20.2 8.9 %collective-permute-start.2 = (bf16[128,1,256]{2,0,1:T(8,128)(2,1)S(1)}, bf16[128,1,256]{2,0,1:T(8,128)(2,1)S(1)}, u32[]{:S(2)}, u32[]{:S(2)}) collective-permute-start(bf16[128,1,256]{2,0,1:T(8,128)(2,1)S(1)} %collective-permute-done), channel_id=1, source_target_pairs={{0,4},{4,8},{8,12},{12,16},{16,20},{20,24},{24,28},{28,32},{32,36}... | collective-permute-start | bytes 196616 | tf_op jit(solution)/shard_map/ppermute | solution.py:18
  22.2 9.2 %collective-permute-start.5 = (bf16[128,1,256]{2,0,1:T(8,128)(2,1)S(1)}, bf16[128,1,256]{2,0,1:T(8,128)(2,1)S(1)}, u32[]{:S(2)}, u32[]{:S(2)}) collective-permute-start(bf16[128,1,256]{2,0,1:T(8,128)(2,1)S(1)} %broadcast_select_fusion.5), channel_id=1, source_target_pairs={{4,0},{8,4},{12,8},{16,12},{20,16},{24,20},{28,24},{32,28},{36,32}... | collective-permute-start | bytes 196616 | tf_op jit(solution)/shard_map/ppermute | solution.py:18
  29.5 8.9 %collective-permute-start.4 = (bf16[128,1,256]{2,0,1:T(8,128)(2,1)S(1)}, bf16[128,1,256]{2,0,1:T(8,128)(2,1)S(1)}, u32[]{:S(2)}, u32[]{:S(2)}) collective-permute-start(bf16[128,1,256]{2,0,1:T(8,128)(2,1)S(1)} %collective-permute-done.2), channel_id=1, source_target_pairs={{0,4},{4,8},{8,12},{12,16},{16,20},{20,24},{24,28},{28,32},{32,36}... | collective-permute-start | bytes 196616 | tf_op jit(solution)/shard_map/ppermute | solution.py:18
  31.4 9.2 %collective-permute-start.7 = (bf16[128,1,256]{2,0,1:T(8,128)(2,1)S(1)}, bf16[128,1,256]{2,0,1:T(8,128)(2,1)S(1)}, u32[]{:S(2)}, u32[]{:S(2)}) collective-permute-start(bf16[128,1,256]{2,0,1:T(8,128)(2,1)S(1)} %broadcast_select_fusion.4), channel_id=1, source_target_pairs={{4,0},{8,4},{12,8},{16,12},{20,16},{24,20},{28,24},{32,28},{36,32}... | collective-permute-start | bytes 196616 | tf_op jit(solution)/shard_map/ppermute | solution.py:18
  38.7 8.9 %collective-permute-start.6 = (bf16[128,1,256]{2,0,1:T(8,128)(2,1)S(1)}, bf16[128,1,256]{2,0,1:T(8,128)(2,1)S(1)}, u32[]{:S(2)}, u32[]{:S(2)}) collective-permute-start(bf16[128,1,256]{2,0,1:T(8,128)(2,1)S(1)} %collective-permute-done.4), channel_id=1, source_target_pairs={{0,4},{4,8},{8,12},{12,16},{16,20},{20,24},{24,28},{28,32},{32,36}... | collective-permute-start | bytes 196616 | tf_op jit(solution)/shard_map/ppermute | solution.py:18
  40.7 9.2 %collective-permute-start.9 = (bf16[128,1,256]{2,0,1:T(8,128)(2,1)S(1)}, bf16[128,1,256]{2,0,1:T(8,128)(2,1)S(1)}, u32[]{:S(2)}, u32[]{:S(2)}) collective-permute-start(bf16[128,1,256]{2,0,1:T(8,128)(2,1)S(1)} %broadcast_select_fusion.3), channel_id=1, source_target_pairs={{4,0},{8,4},{12,8},{16,12},{20,16},{24,20},{28,24},{32,28},{36,32}... | collective-permute-start | bytes 196616 | tf_op jit(solution)/shard_map/ppermute | solution.py:18
  48.0 8.9 %collective-permute-start.8 = (bf16[128,1,256]{2,0,1:T(8,128)(2,1)S(1)}, bf16[128,1,256]{2,0,1:T(8,128)(2,1)S(1)}, u32[]{:S(2)}, u32[]{:S(2)}) collective-permute-start(bf16[128,1,256]{2,0,1:T(8,128)(2,1)S(1)} %collective-permute-done.6), channel_id=1, source_target_pairs={{0,4},{4,8},{8,12},{12,16},{16,20},{20,24},{24,28},{28,32},{32,36}... | collective-permute-start | bytes 196616 | tf_op jit(solution)/shard_map/ppermute | solution.py:18
  49.9 9.2 %collective-permute-start.11 = (bf16[128,1,256]{2,0,1:T(8,128)(2,1)S(1)}, bf16[128,1,256]{2,0,1:T(8,128)(2,1)S(1)}, u32[]{:S(2)}, u32[]{:S(2)}) collective-permute-start(bf16[128,1,256]{2,0,1:T(8,128)(2,1)S(1)} %broadcast_select_fusion.2), channel_id=1, source_target_pairs={{4,0},{8,4},{12,8},{16,12},{20,16},{24,20},{28,24},{32,28},{36,32}... | collective-permute-start | bytes 196616 | tf_op jit(solution)/shard_map/ppermute | solution.py:18
  57.2 8.9 %collective-permute-start.10 = (bf16[128,1,256]{2,0,1:T(8,128)(2,1)S(1)}, bf16[128,1,256]{2,0,1:T(8,128)(2,1)S(1)}, u32[]{:S(2)}, u32[]{:S(2)}) collective-permute-start(bf16[128,1,256]{2,0,1:T(8,128)(2,1)S(1)} %collective-permute-done.8), channel_id=1, source_target_pairs={{0,4},{4,8},{8,12},{12,16},{16,20},{20,24},{24,28},{28,32},{32,36}... | collective-permute-start | bytes 196616 | tf_op jit(solution)/shard_map/ppermute | solution.py:18
  59.2 9.2 %collective-permute-start.13 = (bf16[128,1,256]{2,0,1:T(8,128)(2,1)S(1)}, bf16[128,1,256]{2,0,1:T(8,128)(2,1)S(1)}, u32[]{:S(2)}, u32[]{:S(2)}) collective-permute-start(bf16[128,1,256]{2,0,1:T(8,128)(2,1)S(1)} %broadcast_select_fusion.1), channel_id=1, source_target_pairs={{4,0},{8,4},{12,8},{16,12},{20,16},{24,20},{28,24},{32,28},{36,32}... | collective-permute-start | bytes 196616 | tf_op jit(solution)/shard_map/ppermute | solution.py:18
  66.5 8.9 %collective-permute-start.12 = (bf16[128,1,256]{2,0,1:T(8,128)(2,1)S(1)}, bf16[128,1,256]{2,0,1:T(8,128)(2,1)S(1)}, u32[]{:S(2)}, u32[]{:S(2)}) collective-permute-start(bf16[128,1,256]{2,0,1:T(8,128)(2,1)S(1)} %collective-permute-done.10), channel_id=1, source_target_pairs={{0,4},{4,8},{8,12},{12,16},{16,20},{20,24},{24,28},{28,32},{32,36}... | collective-permute-start | bytes 196616 | tf_op jit(solution)/shard_map/ppermute | solution.py:18
  68.5 9.4 %collective-permute-start.15 = (bf16[128,1,256]{2,0,1:T(8,128)(2,1)S(1)}, bf16[128,1,256]{2,0,1:T(8,128)(2,1)S(1)}, u32[]{:S(2)}, u32[]{:S(2)}) collective-permute-start(bf16[128,1,256]{2,0,1:T(8,128)(2,1)S(1)} %broadcast_select_fusion), channel_id=1, source_target_pairs={{4,0},{8,4},{12,8},{16,12},{20,16},{24,20},{28,24},{32,28},{36,32}... | collective-permute-start | bytes 196616 | tf_op jit(solution)/shard_map/ppermute | solution.py:18
  75.8 8.9 %collective-permute-start.14 = (bf16[128,1,256]{2,0,1:T(8,128)(2,1)S(1)}, bf16[128,1,256]{2,0,1:T(8,128)(2,1)S(1)}, u32[]{:S(2)}, u32[]{:S(2)}) collective-permute-start(bf16[128,1,256]{2,0,1:T(8,128)(2,1)S(1)} %collective-permute-done.12), channel_id=1, source_target_pairs={{0,4},{4,8},{8,12},{12,16},{16,20},{20,24},{24,28},{28,32},{32,36}... | collective-permute-start | bytes 196616 | tf_op jit(solution)/shard_map/ppermute | solution.py:18
  86.9 0.9 copy-start.1
where the time goes:
time: 94.9 us; the launch traced here: 94.3 us
  starting transfers between devices  68.9 us (73%)
  matrix products  8.16 us (9%)
  waiting for transfers between devices  6.81 us (7%)
  other arithmetic  6.79 us (7%)
  local copies, waits for them, and re-layouts  3.01 us (3%)
    ppermute x16, starting transfers between devices, from_behind(): lax.ppermute(value, axis, [(source, source + steps) for source in range(l...  68.9 us
    ppermute x16, waiting for transfers between devices, from_behind(): lax.ppermute(value, axis, [(source, source + steps) for source in range(l...  6.81 us
    dot_general x9, matrix products, attend(): jnp.einsum('sthgn,snhc->sthgc', rounded_weights, key_block[..., head_size...  5.28 us
    dot_general x9, matrix products, attend(): jnp.einsum('sthgc,snhc->sthgn', rotated, key_block[..., :head_size], pref...  2.88 us
  transfers between devices with their start and end apart: 16, of which 1 were waited for; matrix products, arithmetic and copies ran while one was open for 6% of the time, Pallas kernels for 0%

commit v1 on v0

v1 whole, which is shorter than its diff:
```python
import functools
import math

import jax
import jax.numpy as jnp
import numpy as np
from jax import lax
from jax.experimental import pallas as pl
from jax.experimental.pallas import tpu as pltpu
from jax.sharding import PartitionSpec as P

ROPE_BASE = 500000.0
HALF = 128
HEAD = 128
STEPS = 4
LOW = 32
HEADS = 8
ROWS = HALF * HEADS
EXP2_SCALE = math.log2(math.e) / math.sqrt(HEAD)
HIDDEN = float("-inf")
MESH = pl.DeviceIdType.MESH


def angle_table(blocks):
    freq = ROPE_BASE ** (-np.arange(HEAD // 2, dtype=np.float64) * 2.0 / HEAD)
    freq = np.concatenate([freq, freq])

    def both(at):
        angles = at[:, None] * freq[None, :]
        return [np.cos(angles), np.sin(angles)]

    offsets = np.arange(HALF, dtype=np.float64)
    coarse = np.arange(blocks // LOW, dtype=np.float64) * (LOW * HALF)
    fine = np.arange(LOW, dtype=np.float64) * HALF
    return np.concatenate(both(offsets) + both(coarse) + both(fine)).astype(np.float32)


def kernel(
    devices,
    kv_hbm,
    q_hbm,
    lens_hbm,
    table_hbm,
    out,
    kv,
    q,
    lens,
    table,
    cosines,
    sines,
    k_own,
    k_in,
    v_in,
    q_wide,
    q_rot,
    start,
    top,
    total,
    acc,
    local_sem,
    send_sem,
    recv_sem,
    share_sem,
    shared_sem,
):
    index = lax.axis_index("ctx")
    chip, core = index // 2, index % 2
    chips = devices // 2
    other = 2 * chip + 1 - core

    late, early = 1 - core, core

    @pl.when(chip < STEPS)
    def _():
        k_in[0] = jnp.zeros_like(k_in[0])
        v_in[0] = jnp.zeros_like(v_in[0])

    barrier = pltpu.get_barrier_semaphore()
    pl.semaphore_signal(barrier, inc=1, device_id={"ctx": other}, device_id_type=MESH)

    @pl.when(chip < chips - 1)
    def _():
        pl.semaphore_signal(barrier, inc=1, device_id={"ctx": index + 2}, device_id_type=MESH)

    @pl.when(chip > 0)
    def _():
        pl.semaphore_signal(barrier, inc=1, device_id={"ctx": index - 2}, device_id_type=MESH)

    fetches = [
        pltpu.make_async_copy(src, dst, local_sem.at[i])
        for i, (src, dst) in enumerate(((kv_hbm, kv), (table_hbm, table), (lens_hbm, lens), (q_hbm, q)))
    ]
    for fetch in fetches:
        fetch.start()

    def k_part(stream, stage):
        return k_in.at[stream, stage, pl.ds(0, HALF)]

    def v_part(stream, stage):
        return v_in.at[stream, stage, pl.ds(0, HALF)]

    def own_v(stream):
        return kv.at[pl.ds(pl.multiple_of(stream * HALF, HALF), HALF), pl.ds(HEAD, HEAD)]

    folds = chip == chips - 1

    def onward(what, stream, stage, source):
        inbox = (k_in, v_in)[what]
        fold = jnp.logical_and(folds, stream == 0)
        target = jnp.where(fold, other, jnp.where(stream == 0, index + 2, index - 2))
        to = jnp.where(fold, 1, stream)
        return pltpu.make_async_remote_copy(
            src_ref=source,
            dst_ref=inbox.at[to, stage, pl.ds(0, HALF)],
            send_sem=send_sem.at[stream, what, stage],
            recv_sem=recv_sem.at[to, what, stage],
            device_id={"ctx": target},
            device_id_type=MESH,
        )

    def arrival(what, stream, stage):
        inbox = (k_in, v_in)[what].at[stream, stage - 1, pl.ds(0, HALF)]
        return pltpu.make_async_copy(inbox, inbox, recv_sem.at[stream, what, stage - 1])

    def sharing(what, stream, slot, source):
        inbox = (k_in, v_in)[what]
        return pltpu.make_async_remote_copy(
            src_ref=source,
            dst_ref=inbox.at[stream, slot, pl.ds(HALF, HALF)],
            send_sem=share_sem.at[stream, what, slot],
            recv_sem=shared_sem.at[stream, what, slot],
            device_id={"ctx": other},
            device_id_type=MESH,
        )

    def shared(what, stream, slot):
        inbox = (k_in, v_in)[what].at[stream, slot, pl.ds(HALF, HALF)]
        return pltpu.make_async_copy(inbox, inbox, shared_sem.at[stream, what, slot])

    def goes_on(stream):
        return jnp.logical_or(stream == 0, chip > 0)

    def comes(stream, stage):
        return jnp.logical_or(stream == 1, chip >= stage)

    def send_own(what, stream, source):
        @pl.when(goes_on(stream))
        def _():
            onward(what, stream, 0, source).start()

    def take(what, stage):
        part = (k_part, v_part)[what]
        for stream in (late, early):
            source = part(stream, stage - 1)

            @pl.when(comes(stream, stage))
            def _():
                arrival(what, stream, stage).wait()

                @pl.when(jnp.logical_and(goes_on(stream), stage < STEPS))
                def _():
                    onward(what, stream, stage, source).start()

                if stream is late:
                    sharing(what, stream, stage - 1, source).start()
                else:

                    @pl.when(stage < STEPS)
                    def _():
                        sharing(what, stream, stage, source).start()

    def take_shared(stream, slot):
        @pl.when(comes(stream, slot if stream is late else slot + 1))
        def _():
            shared(1, stream, slot).wait()
            shared(0, stream, slot).wait()

    fetches[0].wait()
    peers = 1 + (chip > 0).astype(jnp.int32) + (chip < chips - 1).astype(jnp.int32)
    pl.semaphore_wait(barrier, peers)

    send_own(1, late, own_v(late))
    send_own(1, early, own_v(early))
    sharing(1, early, 0, own_v(early)).start()

    fetches[1].wait()
    lanes = lax.broadcasted_iota(jnp.int32, (1, HEAD), 1)
    sign = jnp.where(lanes < HEAD // 2, -1.0, 1.0)
    coarse_at = 2 * HALF
    coarse_rows = 2 * devices // LOW
    fine_at = coarse_at + 2 * coarse_rows

    def block_of(stream):
        return jnp.where(stream == 0, index, 2 * devices - 1 - index)

    def rotated(vectors, stream):
        return vectors * cosines[stream] + pltpu.roll(vectors, HEAD // 2, 1) * sines[stream]

    for stream in (late, early):
        block = block_of(stream)
        high, low = block // LOW, block % LOW
        cos_high = table[pl.ds(coarse_at + high, 1), :]
        sin_high = table[pl.ds(coarse_at + coarse_rows + high, 1), :]
        cos_low = table[pl.ds(fine_at + low, 1), :]
        sin_low = table[pl.ds(fine_at + LOW + low, 1), :]
        cos_block = cos_high * cos_low - sin_high * sin_low
        sin_block = sin_high * cos_low + cos_high * sin_low
        cos_offset = table[pl.ds(0, HALF), :]
        sin_offset = table[pl.ds(HALF, HALF), :]
        cosines[stream] = cos_block * cos_offset - sin_block * sin_offset
        sines[stream] = (sign * sin_block) * cos_offset + (sign * cos_block) * sin_offset
        keys = kv[pl.ds(pl.multiple_of(stream * HALF, HALF), HALF), pl.ds(0, HEAD)]
        k_own[stream] = rotated(keys.astype(jnp.float32), stream).astype(jnp.bfloat16)
        send_own(0, stream, k_own.at[stream])
        if stream is early:
            sharing(0, early, 0, k_own.at[early]).start()

    fetches[2].wait()
    lengths = jnp.broadcast_to(lens[...].astype(jnp.float32), (HALF, HALF))
    row = lax.broadcasted_iota(jnp.int32, (HALF, HALF), 0)
    column = lax.broadcasted_iota(jnp.int32, (HALF, HALF), 1)
    ends = jnp.sum(jnp.where(column <= row, lengths, 0.0), axis=1, keepdims=True)
    for stream in (late, early):
        place = (block_of(stream) * HALF + column).astype(jnp.float32)
        start[stream] = jnp.max(jnp.where(ends <= place, ends, 0.0), axis=0, keepdims=True)

    fetches[3].wait()
    for stream in (late, early):
        q_wide[...] = q[pl.ds(pl.multiple_of(stream * ROWS, ROWS), ROWS), :].astype(jnp.float32)
        for head in range(HEADS):
            vectors = q_wide[pl.ds(head, HALF, stride=HEADS), :]
            q_rot[stream, pl.ds(head * HALF, HALF), :] = rotated(vectors, stream).astype(jnp.bfloat16)

    def attend(stream, keys, values, hidden, first):
        flipped = values.T
        for pair in range(HEADS // 2):
            queries = q_rot[stream, pl.ds(pair * 2 * HALF, 2 * HALF), :]
            scores = lax.dot_general(
                keys, queries, (((1,), (1,)), ((), ())), preferred_element_type=jnp.float32
            )
            parts, factors = [], []
            for at in range(2):
                head = 2 * pair + at
                mine = scores[:, at * HALF : (at + 1) * HALF] + hidden
                largest = jnp.max(mine, axis=0, keepdims=True)
                if first:
                    new_top = largest
                else:
                    old_top = top[stream, pl.ds(head, 1), :]
                    new_top = jnp.maximum(old_top, largest)
                    factor = jnp.exp2((old_top - new_top) * EXP2_SCALE)
                    factors.append(factor)
                weights = jnp.exp2((mine - new_top) * EXP2_SCALE)
                added = jnp.sum(weights, axis=0, keepdims=True)
                if not first:
                    added = total[stream, pl.ds(head, 1), :] * factor + added
                top[stream, pl.ds(head, 1), :] = new_top
                total[stream, pl.ds(head, 1), :] = added
                parts.append(weights.astype(jnp.bfloat16))
            product = jnp.dot(flipped, jnp.concatenate(parts, axis=1), preferred_element_type=jnp.float32)
            columns = pl.ds(pair * 2 * HALF, 2 * HALF)
            if first:
                acc[stream, :, columns] = product
            else:
                acc[stream, :, columns] = acc[stream, :, columns] * jnp.concatenate(factors, axis=1) + product

    def attend_own(stream):
        place = (block_of(stream) * HALF + row).astype(jnp.float32)
        visible = jnp.logical_and(row <= column, place >= start[stream])
        values = kv[pl.ds(pl.multiple_of(stream * HALF, HALF), HALF), pl.ds(HEAD, HEAD)]
        attend(stream, k_own[stream], values, jnp.where(visible, 0.0, HIDDEN), True)

    rows_of_two = lax.broadcasted_iota(jnp.int32, (2 * HALF, HALF), 0)

    def attend_step(stream, step):
        take_shared(stream, step - 1)
        place = ((block_of(stream) - 2 * step) * HALF + rows_of_two).astype(jnp.float32)
        hidden = jnp.where(place >= start[stream], 0.0, HIDDEN)
        attend(stream, k_in[stream, step - 1], v_in[stream, step - 1], hidden, False)

    take(1, 1)
    attend_own(late)
    attend_own(early)
    take(0, 1)

    @pl.loop(1, STEPS)
    def _(step):
        attend_step(late, step)
        take(1, step + 1)
        attend_step(early, step)
        take(0, step + 1)

    def finish(stream):
        for head in range(HEADS):
            columns = pl.ds(head * HALF, HALF)
            scaled = acc[stream, :, columns] * (1.0 / total[stream, pl.ds(head, 1), :])
            q_wide[pl.ds(head, HALF, stride=HEADS), :] = scaled.T
        rows = pl.ds(pl.multiple_of(stream * ROWS, ROWS), ROWS)
        out[rows, :] = q_wide[...].astype(jnp.bfloat16)

    attend_step(late, STEPS)
    finish(late)
    attend_step(early, STEPS)
    finish(early)

    for what in (0, 1):
        for stream in (late, early):
            for stage in range(STEPS):

                @pl.when(jnp.logical_and(goes_on(stream), comes(stream, stage)))
                def _():
                    onward(what, stream, stage, (k_part, v_part)[what](stream, stage)).wait_send()

                @pl.when(comes(stream, stage + 1 if stream is late else stage))
                def _():
                    sharing(what, stream, stage, (k_part, v_part)[what](stream, stage)).wait_send()


def shards(table, key_value, queries, doc_lengths):
    devices = lax.axis_size("ctx")
    tokens = key_value.shape[0]
    outside = pl.BlockSpec(memory_space=pltpu.HBM)
    result = pl.pallas_call(
        functools.partial(kernel, devices),
        out_shape=pltpu.VMEM((tokens * HEADS, HEAD), jnp.bfloat16),
        in_specs=[outside] * 4,
        out_specs=pl.BlockSpec(memory_space=pltpu.VMEM),
        scratch_shapes=[
            pltpu.VMEM((2 * HALF, 2 * HEAD), jnp.bfloat16),
            pltpu.VMEM((2 * ROWS, HEAD), jnp.bfloat16),
            pltpu.VMEM((1, HALF), jnp.int32),
            pltpu.VMEM(table.shape, jnp.float32),
            pltpu.VMEM((2, HALF, HEAD), jnp.float32),
            pltpu.VMEM((2, HALF, HEAD), jnp.float32),
            pltpu.VMEM((2, HALF, HEAD), jnp.bfloat16),
            pltpu.VMEM((2, STEPS, 2 * HALF, HEAD), jnp.bfloat16),
            pltpu.VMEM((2, STEPS, 2 * HALF, HEAD), jnp.bfloat16),
            pltpu.VMEM((ROWS, HEAD), jnp.float32),
            pltpu.VMEM((2, ROWS, HEAD), jnp.bfloat16),
            pltpu.VMEM((2, 1, HALF), jnp.float32),
            pltpu.VMEM((2, HEADS, HALF), jnp.float32),
            pltpu.VMEM((2, HEADS, HALF), jnp.float32),
            pltpu.VMEM((2, HEAD, ROWS), jnp.float32),
            pltpu.SemaphoreType.DMA((4,)),
            pltpu.SemaphoreType.DMA((2, 2, STEPS)),
            pltpu.SemaphoreType.DMA((2, 2, STEPS)),
            pltpu.SemaphoreType.DMA((2, 2, STEPS)),
            pltpu.SemaphoreType.DMA((2, 2, STEPS)),
        ],
        compiler_params=pltpu.CompilerParams(
            collective_id=0, has_side_effects=True, vmem_limit_bytes=56 * 2**20
        ),
    )(
        key_value.reshape(tokens, 2 * HEAD),
        queries.reshape(tokens * HEADS, HEAD),
        doc_lengths.reshape(1, HALF),
        table,
    )
    return result.reshape(tokens, HEADS, HEAD)


def solution(mesh):
    table = angle_table(2 * mesh.shape["ctx"])
    in_specs = (P(), P("ctx", "tp", None), P("ctx", "tp", None), P())
    mapped = jax.shard_map(
        shards, mesh=mesh, in_specs=in_specs, out_specs=P("ctx", "tp", None), check_vma=False
    )
    return lambda key_value, queries, doc_lengths: mapped(
        jnp.asarray(table), key_value, queries, doc_lengths
    )
```

time: 94.9 us -> 32.8 us (0.35)
  the two profiles are of different devices: /device:TPU:770 before, /device:TPU:1 now
where the time goes in v1:
time: 32.8 us; the launch traced here: 32.6 us
  Pallas kernels  31.8 us (97%)
  local copies, waits for them, and re-layouts  0.8 us (2%)
    pallas_call x1, Pallas kernels, shards(): pl.pallas_call(functools.partial(kernel, devices), out_shape=pltpu.VMEM((...  31.8 us
    unnamed x1, local copies, waits for them, and re-layouts  0.8 us

profile of v1, /device:TPU:1, one launch (start us, length us, event | category | flops | bytes accessed | tf_op | source)
XLA Modules:
  0.0 32.6 jit_solution(12403484361050868814)
XLA Ops:
  0.0 31.8 %shard_map.46 = bf16[2048,128]{1,0:T(8,128)(2,1)S(1)} custom-call(bf16[256,256]{1,0:T(8,128)(2,1)} %bitcast.6, bf16[2048,128]{1,0:T(8,128)(2,1)} %bitcast.5, s32[1,128]{1,0:T(1,128)} %bitcast.7, f32[352,128]{1,0:T(8,128)} %constant.2.clone.table_hbm), custom_call_target="tpu_custom_call" | custom-call | tf_op jit(solution)/shard_map/pallas_call | solution.py:323
  31.8 0.8 %copy.6 = bf16[256,8,128]{2,1,0:T(8,128)(2,1)} copy(bf16[256,8,128]{2,1,0:T(8,128)(2,1)S(1)} %bitcast.4) | data formatting | bytes 1048576

commit v2 on v1

v2 whole, which is shorter than its diff:
```python
import functools
import math

import jax
import jax.numpy as jnp
import numpy as np
from jax import lax
from jax.experimental import pallas as pl
from jax.experimental.pallas import tpu as pltpu
from jax.sharding import PartitionSpec as P

ROPE_BASE = 500000.0
HALF = 128
HEAD = 128
STEPS = 4
LOW = 32
HEADS = 8
ROWS = HALF * HEADS
EXP2_SCALE = math.log2(math.e) / math.sqrt(HEAD)
HIDDEN = float("-inf")
MESH = pl.DeviceIdType.MESH


def angle_table(blocks):
    freq = ROPE_BASE ** (-np.arange(HEAD // 2, dtype=np.float64) * 2.0 / HEAD)
    freq = np.concatenate([freq, freq])

    def both(at):
        angles = at[:, None] * freq[None, :]
        return [np.cos(angles), np.sin(angles)]

    offsets = np.arange(HALF, dtype=np.float64)
    coarse = np.arange(blocks // LOW, dtype=np.float64) * (LOW * HALF)
    fine = np.arange(LOW, dtype=np.float64) * HALF
    return np.concatenate(both(offsets) + both(coarse) + both(fine)).astype(np.float32)


def kernel(
    devices,
    kv_hbm,
    q_hbm,
    lens_hbm,
    table_hbm,
    out,
    kv,
    q,
    lens,
    table,
    cosines,
    sines,
    k_own,
    k_in,
    v_in,
    q_wide,
    q_rot,
    start,
    top,
    total,
    acc,
    local_sem,
    send_sem,
    share_sem,
    recv_sem,
):
    index = lax.axis_index("ctx")
    chip, core = index // 2, index % 2
    chips = devices // 2
    other = 2 * chip + 1 - core
    both = jnp.logical_and

    def place_of(stream):
        return jnp.where(stream == 0, chip, 2 * chips - 1 - chip)

    def lane_of(stream):
        return jnp.where(stream == 0, core, 1 - core)

    def block_of(stream):
        return 2 * place_of(stream) + lane_of(stream)

    def at(place, lane):
        rising = place < chips
        return jnp.where(rising, 2 * place + lane, 4 * chips - 1 - 2 * place - lane), jnp.where(rising, 0, 1)

    first, second = index == 0, index == 1
    folded = chip == chips - 1

    @pl.when(chip < STEPS)
    def _():
        k_in[0] = jnp.zeros_like(k_in[0])
        v_in[0] = jnp.zeros_like(v_in[0])

    barrier = pltpu.get_barrier_semaphore()

    def greet(condition, device):
        @pl.when(condition)
        def _():
            pl.semaphore_signal(barrier, inc=1, device_id={"ctx": device}, device_id_type=MESH)

    later = jnp.logical_not(first)
    greet(later, other)
    greet(chip >= 1, index - 2)
    greet(chip >= 2, index - 4)
    greet(chip == 3, index - 6)
    greet(chip == 4, index - 8)
    greet(both(later, chip <= chips - 2), index + 2)
    greet(both(later, chip <= chips - 3), index + 4)
    greet(second, 2)
    greet(second, 4)
    greet(chip == chips - 2, other + 2)
    greet(folded, other - 2)

    fetches = [
        pltpu.make_async_copy(src, dst, local_sem.at[i])
        for i, (src, dst) in enumerate(((kv_hbm, kv), (table_hbm, table), (lens_hbm, lens), (q_hbm, q)))
    ]
    for fetch in fetches:
        fetch.start()

    inboxes = (k_in, v_in)

    def slot_part(what, stream, slot, half):
        return inboxes[what].at[stream, slot, pl.ds(pl.multiple_of(half * HALF, HALF), HALF)]

    def own(what, stream):
        if what == 0:
            return k_own.at[stream]
        return kv.at[pl.ds(pl.multiple_of(stream * HALF, HALF), HALF), pl.ds(HEAD, HEAD)]

    def passing(what, stream, hops, slot, source):
        target, to = at(place_of(stream) + hops, lane_of(stream))
        detour = jnp.where(both(target == 0, to == 1), 1, 0)
        return pltpu.make_async_remote_copy(
            src_ref=source,
            dst_ref=slot_part(what, to, slot, detour),
            send_sem=send_sem.at[stream, what, slot],
            recv_sem=recv_sem.at[detour, to, what, slot],
            device_id={"ctx": target + detour},
            device_id_type=MESH,
        )

    def beside(what, stream, slot, half, source, sem):
        return pltpu.make_async_remote_copy(
            src_ref=source,
            dst_ref=slot_part(what, stream, slot, half),
            send_sem=sem.at[stream, what, slot],
            recv_sem=recv_sem.at[half, stream, what, slot],
            device_id={"ctx": other},
            device_id_type=MESH,
        )

    def arrived(what, stream, slot, half):
        part = slot_part(what, stream, slot, half)
        pltpu.make_async_copy(part, part, recv_sem.at[half, stream, what, slot]).wait()

    def reaches(stream, hops):
        return place_of(stream) + hops < 2 * chips

    def comes(stream, stage):
        return place_of(stream) >= stage

    def comes_beside(stream, slot):
        return place_of(stream) >= slot + 1 - lane_of(stream)

    def shares(stream):
        return jnp.logical_not(both(chip == 0, stream == 1))

    def each_own(what, stream, act):
        source = own(what, stream)
        for slot in (3, 2, 1, 0):
            condition = reaches(stream, slot + 1)
            if slot > 1:
                condition = both(condition, place_of(stream) == 0)

            @pl.when(condition)
            def _():
                act(passing(what, stream, slot + 1, slot, source))

        @pl.when(both(lane_of(stream) == 0, shares(stream)))
        def _():
            act(beside(what, stream, 0, 1, source, share_sem))

    def each_passed(what, stream, act):
        source = slot_part(what, stream, 1, 0)
        for hops in (2, 1):

            @pl.when(both(comes(stream, 3), reaches(stream, hops)))
            def _():
                act(passing(what, stream, hops, hops + 1, source))

    def shared_slot(stream, stage):
        return stage - lane_of(stream)

    def shares_stage(stream, stage):
        return both(shares(stream), shared_slot(stream, stage) < STEPS)

    def take(stream, stage, passes):
        @pl.when(comes(stream, stage))
        def _():
            for what in (1, 0):
                arrived(what, stream, stage - 1, 0)
                if passes:
                    each_passed(what, stream, lambda copy: copy.start())

                @pl.when(shares_stage(stream, stage))
                def _():
                    source = slot_part(what, stream, stage - 1, 0)
                    beside(what, stream, shared_slot(stream, stage), 1, source, share_sem).start()

    def take_beside(stream, slot):
        @pl.when(comes_beside(stream, slot))
        def _():
            arrived(1, stream, slot, 1)
            arrived(0, stream, slot, 1)

    def each_to_first(what, act):
        act(beside(what, 1, 0, 1, own(what, 1), share_sem))
        for slot in range(1, STEPS):
            act(beside(what, 1, slot, 1, slot_part(what, 1, slot - 1, 0), share_sem))
        for slot in range(STEPS):
            act(beside(what, 1, slot, 0, slot_part(what, 1, slot, 1), send_sem))

    fetches[0].wait()
    peers = 5 - (chip == 1).astype(jnp.int32) - second.astype(jnp.int32) - folded.astype(jnp.int32)
    pl.semaphore_wait(barrier, peers)

    @pl.loop(0, 2)
    def _(stream):
        each_own(1, stream, lambda copy: copy.start())

    fetches[1].wait()
    lanes = lax.broadcasted_iota(jnp.int32, (1, HEAD), 1)
    sign = jnp.where(lanes < HEAD // 2, -1.0, 1.0)
    coarse_at = 2 * HALF
    coarse_rows = 2 * devices // LOW
    fine_at = coarse_at + 2 * coarse_rows

    def rotated(vectors, stream):
        return vectors * cosines[stream] + pltpu.roll(vectors, HEAD // 2, 1) * sines[stream]

    @pl.loop(0, 2)
    def _(stream):
        block = block_of(stream)
        high, low = block // LOW, block % LOW
        cos_high = table[pl.ds(coarse_at + high, 1), :]
        sin_high = table[pl.ds(coarse_at + coarse_rows + high, 1), :]
        cos_low = table[pl.ds(fine_at + low, 1), :]
        sin_low = table[pl.ds(fine_at + LOW + low, 1), :]
        cos_block = cos_high * cos_low - sin_high * sin_low
        sin_block = sin_high * cos_low + cos_high * sin_low
        cos_offset = table[pl.ds(0, HALF), :]
        sin_offset = table[pl.ds(HALF, HALF), :]
        cosines[stream] = cos_block * cos_offset - sin_block * sin_offset
        sines[stream] = (sign * sin_block) * cos_offset + (sign * cos_block) * sin_offset
        keys = kv[pl.ds(pl.multiple_of(stream * HALF, HALF), HALF), pl.ds(0, HEAD)]
        k_own[stream] = rotated(keys.astype(jnp.float32), stream).astype(jnp.bfloat16)
        each_own(0, stream, lambda copy: copy.start())

    fetches[2].wait()
    lengths = jnp.broadcast_to(lens[...].astype(jnp.float32), (HALF, HALF))
    row = lax.broadcasted_iota(jnp.int32, (HALF, HALF), 0)
    column = lax.broadcasted_iota(jnp.int32, (HALF, HALF), 1)
    ends = jnp.sum(jnp.where(column <= row, lengths, 0.0), axis=1, keepdims=True)
    for stream in range(2):
        position = (block_of(stream) * HALF + column).astype(jnp.float32)
        start[stream] = jnp.max(jnp.where(ends <= position, ends, 0.0), axis=0, keepdims=True)

    fetches[3].wait()

    @pl.loop(0, 2)
    def _(stream):
        q_wide[...] = q[pl.ds(pl.multiple_of(stream * ROWS, ROWS), ROWS), :].astype(jnp.float32)
        for head in range(HEADS):
            vectors = q_wide[pl.ds(head, HALF, stride=HEADS), :]
            q_rot[stream, pl.ds(head * HALF, HALF), :] = rotated(vectors, stream).astype(jnp.bfloat16)

    def attend(stream, keys, values, hidden, opening):
        flipped = values.T
        for pair in range(HEADS // 2):
            queries = q_rot[stream, pl.ds(pair * 2 * HALF, 2 * HALF), :]
            scores = lax.dot_general(
                keys, queries, (((1,), (1,)), ((), ())), preferred_element_type=jnp.float32
            )
            parts, factors = [], []
            for side in range(2):
                head = 2 * pair + side
                mine = scores[:, side * HALF : (side + 1) * HALF] + hidden
                largest = jnp.max(mine, axis=0, keepdims=True)
                if opening:
                    new_top = largest
                else:
                    old_top = top[stream, pl.ds(head, 1), :]
                    new_top = jnp.maximum(old_top, largest)
                    factor = jnp.exp2((old_top - new_top) * EXP2_SCALE)
                    factors.append(factor)
                weights = jnp.exp2((mine - new_top) * EXP2_SCALE)
                added = jnp.sum(weights, axis=0, keepdims=True)
                if not opening:
                    added = total[stream, pl.ds(head, 1), :] * factor + added
                top[stream, pl.ds(head, 1), :] = new_top
                total[stream, pl.ds(head, 1), :] = added
                parts.append(weights.astype(jnp.bfloat16))
            product = jnp.dot(flipped, jnp.concatenate(parts, axis=1), preferred_element_type=jnp.float32)
            columns = pl.ds(pair * 2 * HALF, 2 * HALF)
            if opening:
                acc[stream, :, columns] = product
            else:
                acc[stream, :, columns] = acc[stream, :, columns] * jnp.concatenate(factors, axis=1) + product

    @pl.loop(0, 2)
    def _(stream):
        position = (block_of(stream) * HALF + row).astype(jnp.float32)
        visible = jnp.logical_and(row <= column, position >= start[stream])
        values = kv[pl.ds(pl.multiple_of(stream * HALF, HALF), HALF), pl.ds(HEAD, HEAD)]
        attend(stream, k_own[stream], values, jnp.where(visible, 0.0, HIDDEN), True)

    @pl.loop(0, 2)
    def _(stream):
        @pl.when(comes(stream, 3))
        def _():
            take(stream, 2, True)

    rows_of_two = lax.broadcasted_iota(jnp.int32, (2 * HALF, HALF), 0)

    waiting = chip <= STEPS

    @pl.loop(0, 2 * STEPS)
    def _(turn):
        step = jnp.where(waiting, turn % STEPS, turn // 2) + 1
        stream = jnp.where(waiting, 1 - turn // STEPS, (1 - core + turn) % 2)

        def untaken(stream):
            return jnp.logical_not(both(step == 2, comes(stream, 3)))

        @pl.when(both(untaken(stream), jnp.logical_or(waiting, turn % 2 == 0)))
        def _():
            take(stream, step, False)

        @pl.when(both(untaken(1 - stream), both(jnp.logical_not(waiting), turn % 2 == 0)))
        def _():
            take(1 - stream, step, False)

        take_beside(stream, step - 1)

        @pl.when(both(second, both(stream == 0, step == 1)))
        def _():
            for what in (1, 0):
                each_to_first(what, lambda copy: copy.start())

        @pl.when(comes_beside(stream, step - 1))
        def _():
            position = ((block_of(stream) - 2 * step) * HALF + rows_of_two).astype(jnp.float32)
            hidden = jnp.where(position >= start[stream], 0.0, HIDDEN)
            attend(stream, k_in[stream, step - 1], v_in[stream, step - 1], hidden, False)

        @pl.when(step == STEPS)
        def _():
            for head in range(HEADS):
                columns = pl.ds(head * HALF, HALF)
                scaled = acc[stream, :, columns] * (1.0 / total[stream, pl.ds(head, 1), :])
                q_wide[pl.ds(head, HALF, stride=HEADS), :] = scaled.T
            out[pl.ds(pl.multiple_of(stream * ROWS, ROWS), ROWS), :] = q_wide[...].astype(jnp.bfloat16)

    for what in (1, 0):

        @pl.loop(0, 2)
        def _(stream):
            each_own(what, stream, lambda copy: copy.wait_send())
            each_passed(what, stream, lambda copy: copy.wait_send())

            @pl.loop(1, STEPS + 1)
            def _(stage):
                @pl.when(both(comes(stream, stage), shares_stage(stream, stage)))
                def _():
                    source = slot_part(what, stream, stage - 1, 0)
                    beside(what, stream, shared_slot(stream, stage), 1, source, share_sem).wait_send()

        @pl.when(second)
        def _():
            each_to_first(what, lambda copy: copy.wait_send())


def shards(table, key_value, queries, doc_lengths):
    devices = lax.axis_size("ctx")
    tokens = key_value.shape[0]
    outside = pl.BlockSpec(memory_space=pltpu.HBM)
    result = pl.pallas_call(
        functools.partial(kernel, devices),
        out_shape=pltpu.VMEM((tokens * HEADS, HEAD), jnp.bfloat16),
        in_specs=[outside] * 4,
        out_specs=pl.BlockSpec(memory_space=pltpu.VMEM),
        scratch_shapes=[
            pltpu.VMEM((2 * HALF, 2 * HEAD), jnp.bfloat16),
            pltpu.VMEM((2 * ROWS, HEAD), jnp.bfloat16),
            pltpu.VMEM((1, HALF), jnp.int32),
            pltpu.VMEM(table.shape, jnp.float32),
            pltpu.VMEM((2, HALF, HEAD), jnp.float32),
            pltpu.VMEM((2, HALF, HEAD), jnp.float32),
            pltpu.VMEM((2, HALF, HEAD), jnp.bfloat16),
            pltpu.VMEM((2, STEPS, 2 * HALF, HEAD), jnp.bfloat16),
            pltpu.VMEM((2, STEPS, 2 * HALF, HEAD), jnp.bfloat16),
            pltpu.VMEM((ROWS, HEAD), jnp.float32),
            pltpu.VMEM((2, ROWS, HEAD), jnp.bfloat16),
            pltpu.VMEM((2, 1, HALF), jnp.float32),
            pltpu.VMEM((2, HEADS, HALF), jnp.float32),
            pltpu.VMEM((2, HEADS, HALF), jnp.float32),
            pltpu.VMEM((2, HEAD, ROWS), jnp.float32),
            pltpu.SemaphoreType.DMA((4,)),
            pltpu.SemaphoreType.DMA((2, 2, STEPS)),
            pltpu.SemaphoreType.DMA((2, 2, STEPS)),
            pltpu.SemaphoreType.DMA((2, 2, 2, STEPS)),
        ],
        compiler_params=pltpu.CompilerParams(
            collective_id=0, has_side_effects=True, vmem_limit_bytes=56 * 2**20
        ),
    )(
        key_value.reshape(tokens, 2 * HEAD),
        queries.reshape(tokens * HEADS, HEAD),
        doc_lengths.reshape(1, HALF),
        table,
    )
    return result.reshape(tokens, HEADS, HEAD)


def solution(mesh):
    table = angle_table(2 * mesh.shape["ctx"])
    in_specs = (P(), P("ctx", "tp", None), P("ctx", "tp", None), P())
    mapped = jax.shard_map(
        shards, mesh=mesh, in_specs=in_specs, out_specs=P("ctx", "tp", None), check_vma=False
    )
    return lambda key_value, queries, doc_lengths: mapped(
        jnp.asarray(table), key_value, queries, doc_lengths
    )
```

time: 32.8 us -> 29.4 us (0.90)
  the two profiles are of different devices: /device:TPU:1 before, /device:TPU:29 now
where the time goes in v2:
time: 29.4 us; the launch traced here: 29.3 us
  Pallas kernels  28.5 us (97%)
  local copies, waits for them, and re-layouts  0.8 us (3%)
    pallas_call x1, Pallas kernels, shards(): pl.pallas_call(functools.partial(kernel, devices), out_shape=pltpu.VMEM((...  28.5 us
    unnamed x1, local copies, waits for them, and re-layouts  0.8 us

profile of v2, /device:TPU:29, one launch (start us, length us, event | category | flops | bytes accessed | tf_op | source)
XLA Modules:
  0.0 29.3 jit_solution(15717923269041273947)
XLA Ops:
  0.0 28.5 %shard_map.46 = bf16[2048,128]{1,0:T(8,128)(2,1)S(1)} custom-call(bf16[256,256]{1,0:T(8,128)(2,1)} %bitcast.6, bf16[2048,128]{1,0:T(8,128)(2,1)} %bitcast.5, s32[1,128]{1,0:T(1,128)} %bitcast.7, f32[352,128]{1,0:T(8,128)} %constant.2.clone.table_hbm), custom_call_target="tpu_custom_call" | custom-call | tf_op jit(solution)/shard_map/pallas_call | solution.py:386
  28.5 0.8 %copy.6 = bf16[256,8,128]{2,1,0:T(8,128)(2,1)} copy(bf16[256,8,128]{2,1,0:T(8,128)(2,1)S(1)} %bitcast.4) | data formatting | bytes 1048576

commit v3 on v2

--- a/solution.py
+++ b/solution.py
@@ -166,6 +166,11 @@
 
     def each_own(what, stream, act):
         source = own(what, stream)
+
+        @pl.when(both(lane_of(stream) == 0, shares(stream)))
+        def _():
+            act(beside(what, stream, 0, 1, source, share_sem))
+
         for slot in (3, 2, 1, 0):
             condition = reaches(stream, slot + 1)
             if slot > 1:
@@ -175,17 +180,11 @@
             def _():
                 act(passing(what, stream, slot + 1, slot, source))
 
-        @pl.when(both(lane_of(stream) == 0, shares(stream)))
-        def _():
-            act(beside(what, stream, 0, 1, source, share_sem))
-
-    def each_passed(what, stream, act):
-        source = slot_part(what, stream, 1, 0)
-        for hops in (2, 1):
-
-            @pl.when(both(comes(stream, 3), reaches(stream, hops)))
-            def _():
-                act(passing(what, stream, hops, hops + 1, source))
+    def passes(stream, stage, hops):
+        return both(both(comes(stream, 3), reaches(stream, hops)), stage == 2)
+
+    def passed(what, stream, hops):
+        return passing(what, stream, hops, hops + 1, slot_part(what, stream, 1, 0))
 
     def shared_slot(stream, stage):
         return stage - lane_of(stream)
@@ -193,18 +192,22 @@
     def shares_stage(stream, stage):
         return both(shares(stream), shared_slot(stream, stage) < STEPS)
 
-    def take(stream, stage, passes):
+    def take(stream, stage):
         @pl.when(comes(stream, stage))
         def _():
             for what in (1, 0):
                 arrived(what, stream, stage - 1, 0)
-                if passes:
-                    each_passed(what, stream, lambda copy: copy.start())
 
                 @pl.when(shares_stage(stream, stage))
                 def _():
                     source = slot_part(what, stream, stage - 1, 0)
                     beside(what, stream, shared_slot(stream, stage), 1, source, share_sem).start()
+
+                for hops in (2, 1):
+
+                    @pl.when(passes(stream, stage, hops))
+                    def _():
+                        passed(what, stream, hops).start()
 
     def take_beside(stream, slot):
         @pl.when(comes_beside(stream, slot))
@@ -259,10 +262,10 @@
     lengths = jnp.broadcast_to(lens[...].astype(jnp.float32), (HALF, HALF))
     row = lax.broadcasted_iota(jnp.int32, (HALF, HALF), 0)
     column = lax.broadcasted_iota(jnp.int32, (HALF, HALF), 1)
-    ends = jnp.sum(jnp.where(column <= row, lengths, 0.0), axis=1, keepdims=True)
+    ends = jnp.sum(jnp.where(row <= column, lengths.T, 0.0), axis=0, keepdims=True)
     for stream in range(2):
-        position = (block_of(stream) * HALF + column).astype(jnp.float32)
-        start[stream] = jnp.max(jnp.where(ends <= position, ends, 0.0), axis=0, keepdims=True)
+        position = (block_of(stream) * HALF + row).astype(jnp.float32)
+        start[stream] = jnp.max(jnp.where(ends <= position, ends, 0.0), axis=1, keepdims=True)
 
     fetches[3].wait()
 
@@ -274,42 +277,36 @@
             q_rot[stream, pl.ds(head * HALF, HALF), :] = rotated(vectors, stream).astype(jnp.bfloat16)
 
     def attend(stream, keys, values, hidden, opening):
-        flipped = values.T
-        for pair in range(HEADS // 2):
-            queries = q_rot[stream, pl.ds(pair * 2 * HALF, 2 * HALF), :]
-            scores = lax.dot_general(
-                keys, queries, (((1,), (1,)), ((), ())), preferred_element_type=jnp.float32
-            )
-            parts, factors = [], []
-            for side in range(2):
-                head = 2 * pair + side
-                mine = scores[:, side * HALF : (side + 1) * HALF] + hidden
-                largest = jnp.max(mine, axis=0, keepdims=True)
-                if opening:
-                    new_top = largest
-                else:
-                    old_top = top[stream, pl.ds(head, 1), :]
-                    new_top = jnp.maximum(old_top, largest)
-                    factor = jnp.exp2((old_top - new_top) * EXP2_SCALE)
-                    factors.append(factor)
-                weights = jnp.exp2((mine - new_top) * EXP2_SCALE)
-                added = jnp.sum(weights, axis=0, keepdims=True)
-                if not opening:
-                    added = total[stream, pl.ds(head, 1), :] * factor + added
-                top[stream, pl.ds(head, 1), :] = new_top
-                total[stream, pl.ds(head, 1), :] = added
-                parts.append(weights.astype(jnp.bfloat16))
-            product = jnp.dot(flipped, jnp.concatenate(parts, axis=1), preferred_element_type=jnp.float32)
-            columns = pl.ds(pair * 2 * HALF, 2 * HALF)
-            if opening:
-                acc[stream, :, columns] = product
-            else:
-                acc[stream, :, columns] = acc[stream, :, columns] * jnp.concatenate(factors, axis=1) + product
+        scores = lax.dot_general(
+            q_rot[stream], keys, (((1,), (1,)), ((), ())), preferred_element_type=jnp.float32
+        )
+        scores = scores + jnp.concatenate([hidden] * HEADS, axis=0)
+        largest = jnp.broadcast_to(jnp.max(scores, axis=1, keepdims=True), (ROWS, HEAD))
+        if opening:
+            new_top = largest
+        else:
+            old_top = top[stream]
+            new_top = jnp.maximum(old_top, largest)
+            factor = jnp.exp2((old_top - new_top) * EXP2_SCALE)
+        parts = [
+            jnp.exp2((scores[:, at : at + HALF] - new_top) * EXP2_SCALE)
+            for at in range(0, keys.shape[0], HALF)
+        ]
+        added = functools.reduce(jnp.add, parts)
+        weights = jnp.concatenate([part.astype(jnp.bfloat16) for part in parts], axis=1)
+        product = jnp.dot(weights, values, preferred_element_type=jnp.float32)
+        top[stream] = new_top
+        if opening:
+            total[stream] = added
+            acc[stream] = product
+        else:
+            total[stream] = total[stream] * factor + added
+            acc[stream] = acc[stream] * factor + product
 
     @pl.loop(0, 2)
     def _(stream):
-        position = (block_of(stream) * HALF + row).astype(jnp.float32)
-        visible = jnp.logical_and(row <= column, position >= start[stream])
+        position = (block_of(stream) * HALF + column).astype(jnp.float32)
+        visible = jnp.logical_and(column <= row, position >= start[stream])
         values = kv[pl.ds(pl.multiple_of(stream * HALF, HALF), HALF), pl.ds(HEAD, HEAD)]
         attend(stream, k_own[stream], values, jnp.where(visible, 0.0, HIDDEN), True)
 
@@ -317,27 +314,31 @@
     def _(stream):
         @pl.when(comes(stream, 3))
         def _():
-            take(stream, 2, True)
-
-    rows_of_two = lax.broadcasted_iota(jnp.int32, (2 * HALF, HALF), 0)
+            take(stream, 2)
+
+    columns_of_two = lax.broadcasted_iota(jnp.int32, (HALF, 2 * HALF), 1)
 
     waiting = chip <= STEPS
+    stage = jnp.maximum(chip, 1)
+    paired, single = 2 * (stage - 1), STEPS + 1 - stage
 
     @pl.loop(0, 2 * STEPS)
     def _(turn):
-        step = jnp.where(waiting, turn % STEPS, turn // 2) + 1
-        stream = jnp.where(waiting, 1 - turn // STEPS, (1 - core + turn) % 2)
+        alone = stage + jnp.where(turn < paired + single, turn - paired, turn - paired - single)
+        step = jnp.where(both(waiting, turn >= paired), alone, turn // 2 + 1)
+        order = jnp.where(turn < paired, 1 - turn % 2, jnp.where(turn < paired + single, 1, 0))
+        stream = jnp.where(waiting, order, (1 - core + turn) % 2)
 
         def untaken(stream):
             return jnp.logical_not(both(step == 2, comes(stream, 3)))
 
         @pl.when(both(untaken(stream), jnp.logical_or(waiting, turn % 2 == 0)))
         def _():
-            take(stream, step, False)
+            take(stream, step)
 
         @pl.when(both(untaken(1 - stream), both(jnp.logical_not(waiting), turn % 2 == 0)))
         def _():
-            take(1 - stream, step, False)
+            take(1 - stream, step)
 
         take_beside(stream, step - 1)
 
@@ -348,16 +349,16 @@
 
         @pl.when(comes_beside(stream, step - 1))
         def _():
-            position = ((block_of(stream) - 2 * step) * HALF + rows_of_two).astype(jnp.float32)
+            position = ((block_of(stream) - 2 * step) * HALF + columns_of_two).astype(jnp.float32)
             hidden = jnp.where(position >= start[stream], 0.0, HIDDEN)
             attend(stream, k_in[stream, step - 1], v_in[stream, step - 1], hidden, False)
 
         @pl.when(step == STEPS)
         def _():
             for head in range(HEADS):
-                columns = pl.ds(head * HALF, HALF)
-                scaled = acc[stream, :, columns] * (1.0 / total[stream, pl.ds(head, 1), :])
-                q_wide[pl.ds(head, HALF, stride=HEADS), :] = scaled.T
+                mine = pl.ds(head * HALF, HALF)
+                summed = jnp.sum(total[stream, mine, :], axis=1, keepdims=True)
+                q_wide[pl.ds(head, HALF, stride=HEADS), :] = acc[stream, mine, :] * (1.0 / summed)
             out[pl.ds(pl.multiple_of(stream * ROWS, ROWS), ROWS), :] = q_wide[...].astype(jnp.bfloat16)
 
     for what in (1, 0):
@@ -365,7 +366,6 @@
         @pl.loop(0, 2)
         def _(stream):
             each_own(what, stream, lambda copy: copy.wait_send())
-            each_passed(what, stream, lambda copy: copy.wait_send())
 
             @pl.loop(1, STEPS + 1)
             def _(stage):
@@ -373,6 +373,12 @@
                 def _():
                     source = slot_part(what, stream, stage - 1, 0)
                     beside(what, stream, shared_slot(stream, stage), 1, source, share_sem).wait_send()
+
+                for hops in (2, 1):
+
+                    @pl.when(passes(stream, stage, hops))
+                    def _():
+                        passed(what, stream, hops).wait_send()
 
         @pl.when(second)
         def _():
@@ -400,10 +406,10 @@
             pltpu.VMEM((2, STEPS, 2 * HALF, HEAD), jnp.bfloat16),
             pltpu.VMEM((ROWS, HEAD), jnp.float32),
             pltpu.VMEM((2, ROWS, HEAD), jnp.bfloat16),
-            pltpu.VMEM((2, 1, HALF), jnp.float32),
-            pltpu.VMEM((2, HEADS, HALF), jnp.float32),
-            pltpu.VMEM((2, HEADS, HALF), jnp.float32),
-            pltpu.VMEM((2, HEAD, ROWS), jnp.float32),
+            pltpu.VMEM((2, HALF, 1), jnp.float32),
+            pltpu.VMEM((2, ROWS, HEAD), jnp.float32),
+            pltpu.VMEM((2, ROWS, HEAD), jnp.float32),
+            pltpu.VMEM((2, ROWS, HEAD), jnp.float32),
             pltpu.SemaphoreType.DMA((4,)),
             pltpu.SemaphoreType.DMA((2, 2, STEPS)),
             pltpu.SemaphoreType.DMA((2, 2, STEPS)),

time: 29.4 us -> 24.7 us (0.84)
  the two profiles are of different devices: /device:TPU:29 before, /device:TPU:38 now
where the time goes in v3:
time: 24.7 us; the launch traced here: 24.5 us
  Pallas kernels  23.7 us (96%)
  local copies, waits for them, and re-layouts  0.8 us (3%)
    pallas_call x1, Pallas kernels, shards(): pl.pallas_call(functools.partial(kernel, devices), out_shape=pltpu.VMEM((...  23.7 us
    unnamed x1, local copies, waits for them, and re-layouts  0.8 us

profile of v3, /device:TPU:38, one launch (start us, length us, event | category | flops | bytes accessed | tf_op | source)
XLA Modules:
  0.0 24.5 jit_solution(14411640391975563608)
XLA Ops:
  0.0 23.7 %shard_map.46 = bf16[2048,128]{1,0:T(8,128)(2,1)S(1)} custom-call(bf16[256,256]{1,0:T(8,128)(2,1)} %bitcast.6, bf16[2048,128]{1,0:T(8,128)(2,1)} %bitcast.5, s32[1,128]{1,0:T(1,128)} %bitcast.7, f32[352,128]{1,0:T(8,128)} %constant.2.clone.table_hbm), custom_call_target="tpu_custom_call" | custom-call | tf_op jit(solution)/shard_map/pallas_call | solution.py:392
  23.7 0.8 %copy.6 = bf16[256,8,128]{2,1,0:T(8,128)(2,1)} copy(bf16[256,8,128]{2,1,0:T(8,128)(2,1)S(1)} %bitcast.4) | data formatting | bytes 1048576

commit v4 on v3

--- a/solution.py
+++ b/solution.py
@@ -164,14 +164,16 @@
     def shares(stream):
         return jnp.logical_not(both(chip == 0, stream == 1))
 
-    def each_own(what, stream, act):
+    def each_own(what, stream, act, slots=(3, 2, 1, 0)):
         source = own(what, stream)
 
-        @pl.when(both(lane_of(stream) == 0, shares(stream)))
-        def _():
-            act(beside(what, stream, 0, 1, source, share_sem))
-
-        for slot in (3, 2, 1, 0):
+        if 0 in slots:
+
+            @pl.when(both(lane_of(stream) == 0, shares(stream)))
+            def _():
+                act(beside(what, stream, 0, 1, source, share_sem))
+
+        for slot in slots:
             condition = reaches(stream, slot + 1)
             if slot > 1:
                 condition = both(condition, place_of(stream) == 0)
@@ -192,10 +194,10 @@
     def shares_stage(stream, stage):
         return both(shares(stream), shared_slot(stream, stage) < STEPS)
 
-    def take(stream, stage):
+    def take(stream, stage, whats=(1, 0)):
         @pl.when(comes(stream, stage))
         def _():
-            for what in (1, 0):
+            for what in whats:
                 arrived(what, stream, stage - 1, 0)
 
                 @pl.when(shares_stage(stream, stage))
@@ -228,7 +230,7 @@
 
     @pl.loop(0, 2)
     def _(stream):
-        each_own(1, stream, lambda copy: copy.start())
+        each_own(1, stream, lambda copy: copy.start(), (3, 2, 1))
 
     fetches[1].wait()
     lanes = lax.broadcasted_iota(jnp.int32, (1, HEAD), 1)
@@ -256,7 +258,12 @@
         sines[stream] = (sign * sin_block) * cos_offset + (sign * cos_block) * sin_offset
         keys = kv[pl.ds(pl.multiple_of(stream * HALF, HALF), HALF), pl.ds(0, HEAD)]
         k_own[stream] = rotated(keys.astype(jnp.float32), stream).astype(jnp.bfloat16)
-        each_own(0, stream, lambda copy: copy.start())
+        each_own(0, stream, lambda copy: copy.start(), (3, 2, 1))
+
+    @pl.loop(0, 2)
+    def _(stream):
+        each_own(1, stream, lambda copy: copy.start(), (0,))
+        each_own(0, stream, lambda copy: copy.start(), (0,))
 
     fetches[2].wait()
     lengths = jnp.broadcast_to(lens[...].astype(jnp.float32), (HALF, HALF))
@@ -310,15 +317,17 @@
         values = kv[pl.ds(pl.multiple_of(stream * HALF, HALF), HALF), pl.ds(HEAD, HEAD)]
         attend(stream, k_own[stream], values, jnp.where(visible, 0.0, HIDDEN), True)
 
-    @pl.loop(0, 2)
-    def _(stream):
-        @pl.when(comes(stream, 3))
-        def _():
-            take(stream, 2)
+    for what in (1, 0):
+
+        @pl.loop(0, 2)
+        def _(stream):
+            @pl.when(comes(stream, 3))
+            def _():
+                take(stream, 2, (what,))
 
     columns_of_two = lax.broadcasted_iota(jnp.int32, (HALF, 2 * HALF), 1)
 
-    waiting = chip <= STEPS
+    waiting = jnp.logical_or(both(chip <= STEPS, lax.axis_index("tp") == 0), second)
     stage = jnp.maximum(chip, 1)
     paired, single = 2 * (stage - 1), STEPS + 1 - stage
 
@@ -332,11 +341,13 @@
         def untaken(stream):
             return jnp.logical_not(both(step == 2, comes(stream, 3)))
 
-        @pl.when(both(untaken(stream), jnp.logical_or(waiting, turn % 2 == 0)))
+        single_file = both(waiting, turn >= paired)
+
+        @pl.when(both(untaken(stream), jnp.logical_or(single_file, turn % 2 == 0)))
         def _():
             take(stream, step)
 
-        @pl.when(both(untaken(1 - stream), both(jnp.logical_not(waiting), turn % 2 == 0)))
+        @pl.when(both(untaken(1 - stream), both(jnp.logical_not(single_file), turn % 2 == 0)))
         def _():
             take(1 - stream, step)
 

time: 24.7 us -> 23.6 us (0.955)
  the two profiles are of different devices: /device:TPU:38 before, /device:TPU:4 now
where the time goes in v4:
time: 23.6 us; the launch traced here: 23.4 us
  Pallas kernels  22.6 us (96%)
  local copies, waits for them, and re-layouts  0.8 us (3%)
    pallas_call x1, Pallas kernels, shards(): pl.pallas_call(functools.partial(kernel, devices), out_shape=pltpu.VMEM((...  22.6 us
    unnamed x1, local copies, waits for them, and re-layouts  0.8 us

profile of v4, /device:TPU:4, one launch (start us, length us, event | category | flops | bytes accessed | tf_op | source)
XLA Modules:
  0.0 23.4 jit_solution(14873304059201130179)
XLA Ops:
  0.0 22.6 %shard_map.46 = bf16[2048,128]{1,0:T(8,128)(2,1)S(1)} custom-call(bf16[256,256]{1,0:T(8,128)(2,1)} %bitcast.6, bf16[2048,128]{1,0:T(8,128)(2,1)} %bitcast.5, s32[1,128]{1,0:T(1,128)} %bitcast.7, f32[352,128]{1,0:T(8,128)} %constant.2.clone.table_hbm), custom_call_target="tpu_custom_call" | custom-call | tf_op jit(solution)/shard_map/pallas_call | solution.py:403
  22.6 0.8 %copy.6 = bf16[256,8,128]{2,1,0:T(8,128)(2,1)} copy(bf16[256,8,128]{2,1,0:T(8,128)(2,1)S(1)} %bitcast.4) | data formatting | bytes 1048576

commit v5 on v4

--- a/solution.py
+++ b/solution.py
@@ -217,12 +217,16 @@
             arrived(1, stream, slot, 1)
             arrived(0, stream, slot, 1)
 
-    def each_to_first(what, act):
-        act(beside(what, 1, 0, 1, own(what, 1), share_sem))
-        for slot in range(1, STEPS):
-            act(beside(what, 1, slot, 1, slot_part(what, 1, slot - 1, 0), share_sem))
-        for slot in range(STEPS):
-            act(beside(what, 1, slot, 0, slot_part(what, 1, slot, 1), send_sem))
+    def each_to_first(what, stage, act):
+        @pl.when(stage == 1)
+        def _():
+            act(beside(what, 1, 0, 1, own(what, 1), share_sem))
+
+        @pl.when(stage < STEPS)
+        def _():
+            act(beside(what, 1, stage, 1, slot_part(what, 1, stage - 1, 0), share_sem))
+
+        act(beside(what, 1, stage - 1, 0, slot_part(what, 1, stage - 1, 1), send_sem))
 
     fetches[0].wait()
     peers = 5 - (chip == 1).astype(jnp.int32) - second.astype(jnp.int32) - folded.astype(jnp.int32)
@@ -230,7 +234,11 @@
 
     @pl.loop(0, 2)
     def _(stream):
-        each_own(1, stream, lambda copy: copy.start(), (3, 2, 1))
+        @pl.when(place_of(stream) == 0)
+        def _():
+            each_own(1, stream, lambda copy: copy.start(), (0,))
+
+        each_own(1, stream, lambda copy: copy.start(), (1, 2, 3))
 
     fetches[1].wait()
     lanes = lax.broadcasted_iota(jnp.int32, (1, HEAD), 1)
@@ -258,12 +266,19 @@
         sines[stream] = (sign * sin_block) * cos_offset + (sign * cos_block) * sin_offset
         keys = kv[pl.ds(pl.multiple_of(stream * HALF, HALF), HALF), pl.ds(0, HEAD)]
         k_own[stream] = rotated(keys.astype(jnp.float32), stream).astype(jnp.bfloat16)
-        each_own(0, stream, lambda copy: copy.start(), (3, 2, 1))
+
+        @pl.when(place_of(stream) == 0)
+        def _():
+            each_own(0, stream, lambda copy: copy.start(), (0,))
+
+        each_own(0, stream, lambda copy: copy.start(), (1, 2, 3))
 
     @pl.loop(0, 2)
     def _(stream):
-        each_own(1, stream, lambda copy: copy.start(), (0,))
-        each_own(0, stream, lambda copy: copy.start(), (0,))
+        @pl.when(place_of(stream) > 0)
+        def _():
+            each_own(1, stream, lambda copy: copy.start(), (0,))
+            each_own(0, stream, lambda copy: copy.start(), (0,))
 
     fetches[2].wait()
     lengths = jnp.broadcast_to(lens[...].astype(jnp.float32), (HALF, HALF))
@@ -327,7 +342,8 @@
 
     columns_of_two = lax.broadcasted_iota(jnp.int32, (HALF, 2 * HALF), 1)
 
-    waiting = jnp.logical_or(both(chip <= STEPS, lax.axis_index("tp") == 0), second)
+    late = lax.axis_index("tp") == 0
+    waiting = jnp.logical_or(both(chip <= STEPS, late), second)
     stage = jnp.maximum(chip, 1)
     paired, single = 2 * (stage - 1), STEPS + 1 - stage
 
@@ -351,12 +367,27 @@
         def _():
             take(1 - stream, step)
 
-        take_beside(stream, step - 1)
-
-        @pl.when(both(second, both(stream == 0, step == 1)))
+        from_first = both(stream == 0, step == 1)
+
+        @pl.when(both(second, jnp.where(late, from_first, turn == 0)))
+        def _():
+            take_beside(0, 0)
+
+        @pl.when(jnp.logical_not(both(second, stream == 0)))
+        def _():
+            take_beside(stream, step - 1)
+
+        @pl.when(both(second, both(late, from_first)))
+        def _():
+            @pl.loop(1, STEPS + 1)
+            def _(stage):
+                for what in (1, 0):
+                    each_to_first(what, stage, lambda copy: copy.start())
+
+        @pl.when(both(second, both(jnp.logical_not(late), stream == 1)))
         def _():
             for what in (1, 0):
-                each_to_first(what, lambda copy: copy.start())
+                each_to_first(what, step, lambda copy: copy.start())
 
         @pl.when(comes_beside(stream, step - 1))
         def _():
@@ -393,7 +424,10 @@
 
         @pl.when(second)
         def _():
-            each_to_first(what, lambda copy: copy.wait_send())
+
+            @pl.loop(1, STEPS + 1)
+            def _(stage):
+                each_to_first(what, stage, lambda copy: copy.wait_send())
 
 
 def shards(table, key_value, queries, doc_lengths):

time: 23.6 us -> 22.8 us (0.966)
  the two profiles are of different devices: /device:TPU:4 before, /device:TPU:770 now
where the time goes in v5:
time: 22.8 us; the launch traced here: 22.4 us
  Pallas kernels  21.6 us (95%)
  local copies, waits for them, and re-layouts  0.8 us (4%)
    pallas_call x1, Pallas kernels, shards(): pl.pallas_call(functools.partial(kernel, devices), out_shape=pltpu.VMEM((...  21.6 us
    unnamed x1, local copies, waits for them, and re-layouts  0.8 us

profile of v5, /device:TPU:770, one launch (start us, length us, event | category | flops | bytes accessed | tf_op | source)
XLA Modules:
  0.0 22.4 jit_solution(6449019984156164427)
XLA Ops:
  0.0 21.6 %shard_map.46 = bf16[2048,128]{1,0:T(8,128)(2,1)S(1)} custom-call(bf16[256,256]{1,0:T(8,128)(2,1)} %bitcast.6, bf16[2048,128]{1,0:T(8,128)(2,1)} %bitcast.5, s32[1,128]{1,0:T(1,128)} %bitcast.7, f32[352,128]{1,0:T(8,128)} %constant.2.clone.table_hbm), custom_call_target="tpu_custom_call" | custom-call | tf_op jit(solution)/shard_map/pallas_call | solution.py:437
  21.6 0.8 %copy.6 = bf16[256,8,128]{2,1,0:T(8,128)(2,1)} copy(bf16[256,8,128]{2,1,0:T(8,128)(2,1)S(1)} %bitcast.4) | data formatting | bytes 1048576

commit v6 on v5

--- a/solution.py
+++ b/solution.py
@@ -367,6 +367,34 @@
         def _():
             take(1 - stream, step)
 
+        @pl.when(turn == 2 * STEPS - 1)
+        def _():
+            for what in (1, 0):
+
+                @pl.loop(0, 2)
+                def _(stream):
+                    each_own(what, stream, lambda copy: copy.wait_send())
+
+                    @pl.loop(1, STEPS + 1)
+                    def _(stage):
+                        @pl.when(both(comes(stream, stage), shares_stage(stream, stage)))
+                        def _():
+                            source = slot_part(what, stream, stage - 1, 0)
+                            beside(what, stream, shared_slot(stream, stage), 1, source, share_sem).wait_send()
+
+                        for hops in (2, 1):
+
+                            @pl.when(passes(stream, stage, hops))
+                            def _():
+                                passed(what, stream, hops).wait_send()
+
+                @pl.when(second)
+                def _():
+
+                    @pl.loop(1, STEPS + 1)
+                    def _(stage):
+                        each_to_first(what, stage, lambda copy: copy.wait_send())
+
         from_first = both(stream == 0, step == 1)
 
         @pl.when(both(second, jnp.where(late, from_first, turn == 0)))
@@ -402,32 +430,6 @@
                 summed = jnp.sum(total[stream, mine, :], axis=1, keepdims=True)
                 q_wide[pl.ds(head, HALF, stride=HEADS), :] = acc[stream, mine, :] * (1.0 / summed)
             out[pl.ds(pl.multiple_of(stream * ROWS, ROWS), ROWS), :] = q_wide[...].astype(jnp.bfloat16)
-
-    for what in (1, 0):
-
-        @pl.loop(0, 2)
-        def _(stream):
-            each_own(what, stream, lambda copy: copy.wait_send())
-
-            @pl.loop(1, STEPS + 1)
-            def _(stage):
-                @pl.when(both(comes(stream, stage), shares_stage(stream, stage)))
-                def _():
-                    source = slot_part(what, stream, stage - 1, 0)
-                    beside(what, stream, shared_slot(stream, stage), 1, source, share_sem).wait_send()
-
-                for hops in (2, 1):
-
-                    @pl.when(passes(stream, stage, hops))
-                    def _():
-                        passed(what, stream, hops).wait_send()
-
-        @pl.when(second)
-        def _():
-
-            @pl.loop(1, STEPS + 1)
-            def _(stage):
-                each_to_first(what, stage, lambda copy: copy.wait_send())
 
 
 def shards(table, key_value, queries, doc_lengths):

time: 22.8 us -> 22.7 us (level)
  no operation moved by 1% of the time
where the time goes in v6:
time: 22.7 us; the launch traced here: 22.4 us
  Pallas kernels  21.6 us (95%)
  local copies, waits for them, and re-layouts  0.8 us (4%)
    pallas_call x1, Pallas kernels, shards(): pl.pallas_call(functools.partial(kernel, devices), out_shape=pltpu.VMEM((...  21.6 us
    unnamed x1, local copies, waits for them, and re-layouts  0.8 us

profile of v6, /device:TPU:770, one launch (start us, length us, event | category | flops | bytes accessed | tf_op | source)
XLA Modules:
  0.0 22.4 jit_solution(7094526438853479505)
XLA Ops:
  0.0 21.6 %shard_map.46 = bf16[2048,128]{1,0:T(8,128)(2,1)S(1)} custom-call(bf16[256,256]{1,0:T(8,128)(2,1)} %bitcast.6, bf16[2048,128]{1,0:T(8,128)(2,1)} %bitcast.5, s32[1,128]{1,0:T(1,128)} %bitcast.7, f32[352,128]{1,0:T(8,128)} %constant.2.clone.table_hbm), custom_call_target="tpu_custom_call" | custom-call | tf_op jit(solution)/shard_map/pallas_call | solution.py:439
  21.6 0.8 %copy.6 = bf16[256,8,128]{2,1,0:T(8,128)(2,1)} copy(bf16[256,8,128]{2,1,0:T(8,128)(2,1)S(1)} %bitcast.4) | data formatting | bytes 1048576
